TPU v7x, 32 devices: a whole 2x2x4 slice. The times are simulated.
32 devices in a mesh: groups: 2 (over x), ctx: 16 (over z, y, core).
Axes of the slice: x: 2, y: 2, z: 4, core: 2. Of those that a mesh axis runs over, the one named last changes fastest.
Arguments:
- hidden: bfloat16 [4096, 16384], P(('groups', 'ctx')), parts along dimension 0, may hold values from -6 to 6
- norm_gain: float32 [16384], replicated, may hold values from 0.1 to 1.9
- w_key: bfloat16 [16384, 512], P('ctx'), may hold values from -0.046875 to 0.046875
- w_value: bfloat16 [16384, 512], P('ctx'), may hold values from -0.046875 to 0.046875
- query: bfloat16 [4096, 8192], P(('groups', 'ctx')), parts along dimension 0, may hold values from -256 to 256
- block_order: int32 [64], P('groups'), parts along dimension 0, may hold values from 0 to 31, each once
Outputs:
- attended: bfloat16 [4096, 8192], P(('groups', 'ctx')), parts along dimension 0
There are 2 independent parts, one for each index of `groups`. A program takes and returns all parts, laid end to end along the dimension named above; an argument that names none is the same for every part. Nothing has to cross between parts.
Inputs may be any that keep to these rules, and one draw needn't show every extreme that they name: `block_order`: each number appears once.
All inputs are finite; a program needn't handle non-finite values.
Results may differ from a plain program's by a relative error of at most 0.0045.
The roundings to bfloat16 on the way count: a program that leaves them out, or rounds other values in their place, can miss the bound.
Values may be sent and summed in bfloat16 or wider, within the bound.
A program may use at most 128 MiB of HBM per device.

v0:
```python
import math

import jax
import jax.numpy as jnp
from jax import lax
from jax.sharding import PartitionSpec as P

HD = 128


def lookup(entries, slot_index):
    matches = slot_index[:, None] == jnp.arange(entries.shape[0], dtype=jnp.int32)[None, :]
    return jnp.sum(jnp.where(matches, entries[None, :], 0), axis=1)


def rotate(raw_keys, positions):
    half_width = HD // 2
    freqs = jnp.exp(jnp.arange(half_width, dtype=jnp.float32) * (-2.0 * math.log(500000.0) / HD))
    angles = positions.astype(jnp.float32)[:, None] * freqs[None, :]
    cosine = jnp.cos(angles)[:, None, :]
    sine = jnp.sin(angles)[:, None, :]
    shaped = raw_keys.reshape(raw_keys.shape[0], -1, HD)
    front = shaped[..., :half_width]
    behind = shaped[..., half_width:]
    turned = jnp.concatenate(
        [front * cosine - behind * sine, behind * cosine + front * sine], axis=-1
    )
    return turned.reshape(raw_keys.shape[0], -1)


def body(hidden, norm_gain, w_key, w_value, query, block_order):
    tok_rows = hidden.shape[0]
    half_rows = tok_rows // 2
    kv_width = w_key.shape[1]
    kv_heads = kv_width // HD
    group_size = query.shape[1] // kv_width
    device = lax.axis_index("ctx")
    local_ids = jnp.arange(tok_rows, dtype=jnp.int32)
    own_blocks = lax.dynamic_slice_in_dim(block_order, 2 * device, 2)
    positions = lookup(own_blocks, local_ids // half_rows) * half_rows + local_ids % half_rows
    widened = hidden.astype(jnp.float32)
    mean_square = jnp.mean(widened * widened, axis=1, keepdims=True)
    normed = (widened * lax.rsqrt(mean_square + 1e-05) * norm_gain[None, :]).astype(jnp.bfloat16)
    key_raw = jnp.dot(
        normed, lax.all_gather(w_key, "ctx", axis=0, tiled=True), preferred_element_type=jnp.float32
    )
    value_raw = jnp.dot(
        normed,
        lax.all_gather(w_value, "ctx", axis=0, tiled=True),
        preferred_element_type=jnp.float32,
    )
    keys = rotate(key_raw, positions).astype(jnp.bfloat16)
    values = value_raw.astype(jnp.bfloat16)
    grouped_query = query.reshape(tok_rows, kv_heads, group_size, HD)
    score_scale = 1.0 / math.sqrt(HD)

    def update(state_now, key_block, value_block, key_positions):
        running_max, totals, weighted = state_now
        scores = (
            jnp.einsum(
                "tkgd,skd->tkgs", grouped_query, key_block, preferred_element_type=jnp.float32
            )
            * score_scale
        )
        allowed = key_positions[None, None, None, :] <= positions[:, None, None, None]
        scores = jnp.where(allowed, scores, -1e30)
        new_max = jnp.maximum(running_max, jnp.max(scores, axis=-1))
        weights = jnp.where(allowed, jnp.exp(scores - new_max[..., None]), 0.0)
        rescale = jnp.exp(running_max - new_max)
        totals = totals * rescale + jnp.sum(weights, axis=-1)
        weighted = weighted * rescale[..., None] + jnp.einsum(
            "tkgs,skd->tkgd",
            weights.astype(jnp.bfloat16),
            value_block,
            preferred_element_type=jnp.float32,
        )
        return (new_max, totals, weighted)

    start_state = (
        jnp.full((tok_rows, kv_heads, group_size), -1e30, jnp.float32),
        jnp.zeros((tok_rows, kv_heads, group_size), jnp.float32),
        jnp.zeros((tok_rows, kv_heads, group_size, HD), jnp.float32),
    )
    state_now = start_state
    key_piece = lax.all_gather(keys, "ctx", axis=0, tiled=True)
    value_piece = lax.all_gather(values, "ctx", axis=0, tiled=True)
    row_count = key_piece.shape[0]
    key_ids = jnp.arange(row_count, dtype=jnp.int32)
    key_positions = lookup(block_order, key_ids // half_rows) * half_rows + key_ids % half_rows
    block_width = math.gcd(row_count, 512)
    blocks = row_count // block_width
    key_blocks = key_piece.reshape(blocks, block_width, kv_heads, HD)
    value_blocks = value_piece.reshape(blocks, block_width, kv_heads, HD)
    position_blocks = key_positions.reshape(blocks, block_width)

    def advance(state_inner, item):
        key_block, value_block, block_positions = item
        state_inner = update(state_inner, key_block, value_block, block_positions)
        return (state_inner, None)

    state_now, _ = lax.scan(advance, state_now, (key_blocks, value_blocks, position_blocks))
    final_max, totals, weighted = state_now
    attended = (weighted / totals[..., None]).astype(jnp.bfloat16)
    return attended.reshape(tok_rows, kv_heads * group_size * HD)


def solution(mesh):
    return jax.shard_map(
        body,
        mesh=mesh,
        in_specs=(
            P(("groups", "ctx"), None),
            P(),
            P("ctx", None),
            P("ctx", None),
            P(("groups", "ctx"), None),
            P("groups"),
        ),
        out_specs=P(("groups", "ctx"), None),
        check_vma=False,
    )
```

profile of v0, /device:TPU:0, one launch (start us, length us, event | category | flops | bytes accessed | tf_op | source)
XLA Modules:
  0.0 487.2 jit_solution(17939269906072096382)
XLA Ops:
  6.5 0.0 all-gather.5.cloned.1.call-start
  6.5 0.7 all-gather.5.cloned.1.call-update
  7.3 0.0 all-gather.9.cloned.1.call-start
  7.3 0.7 all-gather.9.cloned.1.call-update
  8.0 0.0 all-gather.7.cloned.1.call-start
  8.1 0.7 dynamic_slice.14
  8.8 0.1 fusion.29
  8.9 3.1 fusion.14
  12.0 0.3 multiply_cosine_fusion
  12.3 0.0 copy-start.2
  12.3 126.8 %all-gather.5.cloned.1.call-done = bf16[16384,512]{1,0:T(8,128)(2,1)} async-done(((bf16[1024,512]{1,0:T(8,128)(2,1)}), bf16[16384,512]{1,0:T(8,128)(2,1)}) %all-gather.5.cloned.1.call-update) | async-done | bytes 16777232 | tf_op jit(solution)/shard_map/all_gather | solution.py:45
  139.1 9.4 %fusion.19 = f32[128,512]{1,0:T(8,128)S(1)} fusion(bf16[16384,512]{1,0:T(8,128)(2,1)} %all-gather.5.cloned.1.call-done, bf16[128,16384]{1,0:T(8,128)(2,1)} %param.8, f32[16384]{0:T(1024)} %param.9, f32[128]{0:T(128)S(1)} %add_rsqrt_fusion), kind=kOutput, calls=%fused_computation.30 | convolution fusion | flops 2155872256 | bytes 21299712 | tf_op jit(solution)/shard_map/dot_general | solution.py:44
  148.6 0.1 reshape.159
  148.7 0.3 subtract_convert_fusion
  149.0 0.2 pad_maximum_fusion
  149.2 0.7 copy.34
  149.9 0.0 all-gather.7.cloned.1.call-update
  149.9 0.0 copy-start
  149.9 0.2 all-gather.11.cloned.1.call-start
  150.1 116.3 %all-gather.9.cloned.1.call-done = bf16[16384,512]{1,0:T(8,128)(2,1)} async-done(((bf16[1024,512]{1,0:T(8,128)(2,1)}), bf16[16384,512]{1,0:T(8,128)(2,1)}) %all-gather.9.cloned.1.call-update) | async-done | bytes 16777232 | tf_op jit(solution)/shard_map/all_gather | solution.py:49
  266.4 0.0 copy-done.2
  266.4 10.1 %fusion.21 = bf16[128,512]{1,0:T(8,128)(2,1)} fusion(bf16[16384,512]{1,0:T(8,128)(2,1)} %all-gather.9.cloned.1.call-done, bf16[128,16384]{1,0:T(8,128)(2,1)} %param.8, f32[16384]{0:T(1024)S(1)} %copy-done.2, f32[128]{0:T(128)S(1)} %add_rsqrt_fusion), kind=kOutput, calls=%fused_computation.31 | convolution fusion | flops 2155937792 | bytes 21168640 | tf_op jit(solution)/shard_map/dot_general | solution.py:47
  276.5 0.0 copy-start.1
  276.5 0.0 all-gather.11.cloned.1.call-update
  276.5 0.0 copy-done
  276.6 2.4 copy.17
  279.0 3.0 copy.19
  282.1 0.0 copy-done.1
  282.1 0.1 select_reduce_fusion
  282.2 26.0 %all-gather.7.cloned.1.call-done = bf16[2048,512]{1,0:T(8,128)(2,1)} async-done(((bf16[128,512]{1,0:T(8,128)(2,1)}), bf16[2048,512]{1,0:T(8,128)(2,1)}) %all-gather.7.cloned.1.call-update) | async-done | bytes 2097168 | tf_op jit(solution)/shard_map/all_gather | solution.py:85
  308.2 4.0 reshape.160
  312.1 38.3 %all-gather.11.cloned.1.call-done = bf16[2048,512]{1,0:T(8,128)(2,1)} async-done(((bf16[128,512]{1,0:T(8,128)(2,1)}), bf16[2048,512]{1,0:T(8,128)(2,1)}) %all-gather.11.cloned.1.call-update) | async-done | bytes 2097168 | tf_op jit(solution)/shard_map/all_gather | solution.py:86
  350.4 4.0 reshape.162
  354.4 120.6 %while.15 = (s32[]{:T(128)}, f32[128,4,16]{0,2,1:T(8,128)S(1)}, f32[128,4,16]{0,2,1:T(8,128)S(1)}, f32[128,4,16,128]{0,3,2,1:T(8,128)}, s32[4,512]{1,0:T(4,128)S...) while((s32[]{:T(128)}, f32[128,4,16]{0,2,1:T(8,128)S(1)}, ...), condition=%wide.region_6.7_spmd.clone, body=%wide.region_3.6_spmd.clone.sunk | while | flops 2205261824 | bytes 65804924 | solution.py:101
  354.4 0.1 broadcast_compare_fusion.2
  354.5 1.6 constant_dynamic-slice_fusion.6
  356.1 7.1 %fusion.45 = (f32[128,4,16]{0,2,1:T(8,128)S(1)}, f32[4,512,128,16]{2,1,3,0:T(8,128)}) fusion(pred[128,512]{0,1:T(8,128)(4,1)S(1)} %broadcast_compare_fusion.2, bf16[128,4,16,128]{3,0,2,1:T(8,128)(2,1)S(1)} %get-tuple-element.238, bf16[1,512,4,128]{3,2,1,0:T(4,128)(2,1)S(1)} %get-tuple-element.203), kind=kOutput, calls=%fused_computation.2.clone.1 | convolution fusion | flops 1086316544 | bytes 19496960 | tf_op jit(solution)/shard_map/while/body/eval_jaxpr/tkgd,skd->tkgs/dot_general | solution.py:60
  363.2 8.0 %fusion.46 = f32[128,4,16]{0,2,1:T(8,128)S(1)} fusion(f32[4,512,128,16]{2,1,3,0:T(8,128)} %get-tuple-element.205, f32[128,4,16]{0,2,1:T(8,128)S(1)} %select_maximum_fusion.2, pred[128,512]{0,1:T(8,128)(4,1)S(1)} %broadcast_compare_fusion.2), kind=kLoop, calls=%fused_computation.4.clone.1 | loop fusion | flops 20963328 | bytes 16908288 | tf_op jit(solution)/shard_map/while/body/eval_jaxpr/reduce_sum | solution.py:70
  371.2 0.3 copy.38
  371.5 12.1 %bitcast_add_fusion.2 = f32[128,4,16,128]{0,3,2,1:T(8,128)} fusion(f32[128,4,16,128]{0,3,2,1:T(8,128)} %get-tuple-element.223, f32[4,512,128,16]{2,1,3,0:T(8,128)} %get-tuple-element.205, f32[128,4,16]{0,2,1:T(8,128)S(1)} %select_maximum_fusion.2, pred[128,512]{0,1:T(8,128)(4,1)S(1)} %broadcast_compare_fusion.2, ...), kind=kOutput, calls=%fused_computation.7.clone.1 | convolution fusion | flops 1097859072 | bytes 25821184 | tf_op jit(solution)/shard_map/while/body/eval_jaxpr/tkgs,skd->tkgd/dot_general | solution.py:71
  383.6 0.1 broadcast_compare_fusion.2
  383.8 1.6 constant_dynamic-slice_fusion.6
  385.4 7.1 %fusion.45 = (f32[128,4,16]{0,2,1:T(8,128)S(1)}, f32[4,512,128,16]{2,1,3,0:T(8,128)}) fusion(pred[128,512]{0,1:T(8,128)(4,1)S(1)} %broadcast_compare_fusion.2, bf16[128,4,16,128]{3,0,2,1:T(8,128)(2,1)S(1)} %get-tuple-element.238, bf16[1,512,4,128]{3,2,1,0:T(4,128)(2,1)S(1)} %get-tuple-element.203), kind=kOutput, calls=%fused_computation.2.clone.1 | convolution fusion | flops 1086316544 | bytes 19496960 | tf_op jit(solution)/shard_map/while/body/eval_jaxpr/tkgd,skd->tkgs/dot_general | solution.py:60
  392.5 8.0 %fusion.46 = f32[128,4,16]{0,2,1:T(8,128)S(1)} fusion(f32[4,512,128,16]{2,1,3,0:T(8,128)} %get-tuple-element.205, f32[128,4,16]{0,2,1:T(8,128)S(1)} %select_maximum_fusion.2, pred[128,512]{0,1:T(8,128)(4,1)S(1)} %broadcast_compare_fusion.2), kind=kLoop, calls=%fused_computation.4.clone.1 | loop fusion | flops 20963328 | bytes 16908288 | tf_op jit(solution)/shard_map/while/body/eval_jaxpr/reduce_sum | solution.py:70
  400.5 0.3 copy.38
  400.8 13.3 %bitcast_add_fusion.2 = f32[128,4,16,128]{0,3,2,1:T(8,128)} fusion(f32[128,4,16,128]{0,3,2,1:T(8,128)} %get-tuple-element.223, f32[4,512,128,16]{2,1,3,0:T(8,128)} %get-tuple-element.205, f32[128,4,16]{0,2,1:T(8,128)S(1)} %select_maximum_fusion.2, pred[128,512]{0,1:T(8,128)(4,1)S(1)} %broadcast_compare_fusion.2, ...), kind=kOutput, calls=%fused_computation.7.clone.1 | convolution fusion | flops 1097859072 | bytes 25821184 | tf_op jit(solution)/shard_map/while/body/eval_jaxpr/tkgs,skd->tkgd/dot_general | solution.py:71
  414.1 0.1 broadcast_compare_fusion.2
  414.2 1.6 constant_dynamic-slice_fusion.6
  415.8 7.1 %fusion.45 = (f32[128,4,16]{0,2,1:T(8,128)S(1)}, f32[4,512,128,16]{2,1,3,0:T(8,128)}) fusion(pred[128,512]{0,1:T(8,128)(4,1)S(1)} %broadcast_compare_fusion.2, bf16[128,4,16,128]{3,0,2,1:T(8,128)(2,1)S(1)} %get-tuple-element.238, bf16[1,512,4,128]{3,2,1,0:T(4,128)(2,1)S(1)} %get-tuple-element.203), kind=kOutput, calls=%fused_computation.2.clone.1 | convolution fusion | flops 1086316544 | bytes 19496960 | tf_op jit(solution)/shard_map/while/body/eval_jaxpr/tkgd,skd->tkgs/dot_general | solution.py:60
  422.9 8.0 %fusion.46 = f32[128,4,16]{0,2,1:T(8,128)S(1)} fusion(f32[4,512,128,16]{2,1,3,0:T(8,128)} %get-tuple-element.205, f32[128,4,16]{0,2,1:T(8,128)S(1)} %select_maximum_fusion.2, pred[128,512]{0,1:T(8,128)(4,1)S(1)} %broadcast_compare_fusion.2), kind=kLoop, calls=%fused_computation.4.clone.1 | loop fusion | flops 20963328 | bytes 16908288 | tf_op jit(solution)/shard_map/while/body/eval_jaxpr/reduce_sum | solution.py:70
  430.9 0.3 copy.38
  431.3 13.3 %bitcast_add_fusion.2 = f32[128,4,16,128]{0,3,2,1:T(8,128)} fusion(f32[128,4,16,128]{0,3,2,1:T(8,128)} %get-tuple-element.223, f32[4,512,128,16]{2,1,3,0:T(8,128)} %get-tuple-element.205, f32[128,4,16]{0,2,1:T(8,128)S(1)} %select_maximum_fusion.2, pred[128,512]{0,1:T(8,128)(4,1)S(1)} %broadcast_compare_fusion.2, ...), kind=kOutput, calls=%fused_computation.7.clone.1 | convolution fusion | flops 1097859072 | bytes 25821184 | tf_op jit(solution)/shard_map/while/body/eval_jaxpr/tkgs,skd->tkgd/dot_general | solution.py:71
  444.6 0.1 broadcast_compare_fusion.2
  444.7 1.6 constant_dynamic-slice_fusion.6
  446.3 7.1 %fusion.45 = (f32[128,4,16]{0,2,1:T(8,128)S(1)}, f32[4,512,128,16]{2,1,3,0:T(8,128)}) fusion(pred[128,512]{0,1:T(8,128)(4,1)S(1)} %broadcast_compare_fusion.2, bf16[128,4,16,128]{3,0,2,1:T(8,128)(2,1)S(1)} %get-tuple-element.238, bf16[1,512,4,128]{3,2,1,0:T(4,128)(2,1)S(1)} %get-tuple-element.203), kind=kOutput, calls=%fused_computation.2.clone.1 | convolution fusion | flops 1086316544 | bytes 19496960 | tf_op jit(solution)/shard_map/while/body/eval_jaxpr/tkgd,skd->tkgs/dot_general | solution.py:60
  453.4 8.0 %fusion.46 = f32[128,4,16]{0,2,1:T(8,128)S(1)} fusion(f32[4,512,128,16]{2,1,3,0:T(8,128)} %get-tuple-element.205, f32[128,4,16]{0,2,1:T(8,128)S(1)} %select_maximum_fusion.2, pred[128,512]{0,1:T(8,128)(4,1)S(1)} %broadcast_compare_fusion.2), kind=kLoop, calls=%fused_computation.4.clone.1 | loop fusion | flops 20963328 | bytes 16908288 | tf_op jit(solution)/shard_map/while/body/eval_jaxpr/reduce_sum | solution.py:70
  461.4 0.3 copy.38
  461.7 13.3 %bitcast_add_fusion.2 = f32[128,4,16,128]{0,3,2,1:T(8,128)} fusion(f32[128,4,16,128]{0,3,2,1:T(8,128)} %get-tuple-element.223, f32[4,512,128,16]{2,1,3,0:T(8,128)} %get-tuple-element.205, f32[128,4,16]{0,2,1:T(8,128)S(1)} %select_maximum_fusion.2, pred[128,512]{0,1:T(8,128)(4,1)S(1)} %broadcast_compare_fusion.2, ...), kind=kOutput, calls=%fused_computation.7.clone.1 | convolution fusion | flops 1097859072 | bytes 25821184 | tf_op jit(solution)/shard_map/while/body/eval_jaxpr/tkgs,skd->tkgd/dot_general | solution.py:71
  475.0 2.8 divide_convert_fusion
  477.8 2.9 copy.25
  (27 shorter events, 0.2 us)
Async XLA Ops:
  6.5 132.6 %all-gather.5.cloned.1.call-start = ((), (), s32[]{:S(2)}) async-start(), calls=%async_computation | async-start | bytes 17825792 | tf_op jit(solution)/shard_map/all_gather | solution.py:45
  7.3 259.1 %all-gather.9.cloned.1.call-start = ((), (), s32[]{:S(2)}) async-start(), calls=%async_computation.2 | async-start | bytes 17825792 | tf_op jit(solution)/shard_map/all_gather | solution.py:49
  8.0 300.2 %all-gather.7.cloned.1.call-start = ((), (), s32[]{:S(2)}) async-start(), calls=%async_computation.1 | async-start | bytes 2228224 | tf_op jit(solution)/shard_map/all_gather | solution.py:85
  12.3 254.1 %copy-start.2 = (f32[16384]{0:T(1024)S(1)}, f32[16384]{0:T(1024)}, u32[]{:S(2)}) copy-start(f32[16384]{0:T(1024)} %param.9) | copy-start | bytes 196612
  149.9 126.7 %copy-start = (bf16[128,8192]{1,0:T(8,128)(2,1)S(1)}, bf16[128,8192]{1,0:T(8,128)(2,1)}, u32[]{:S(2)}) copy-start(bf16[128,8192]{1,0:T(8,128)(2,1)} %param.12) | copy-start | bytes 6291460
  149.9 200.5 %all-gather.11.cloned.1.call-start = ((), (), s32[]{:S(2)}) async-start(), calls=%async_computation.3 | async-start | bytes 2228224 | tf_op jit(solution)/shard_map/all_gather | solution.py:86
  276.5 5.6 %copy-start.1 = (s32[32]{0:T(128)S(1)}, s32[32]{0:T(128)}, u32[]{:S(2)}) copy-start(s32[32]{0:T(128)} %param.13) | copy-start | bytes 388
Sparse Core Ops, SparseCore 0:
  9.5 129.5 all-gather.4
  141.3 125.0 all-gather.8
  268.6 39.5 all-gather.6
  310.2 40.1 all-gather.10
where the time goes:
time: 488 us; the launch traced here: 487 us
  waiting for transfers between devices  309 us (63%)
  matrix products  99.9 us (20%)
  other arithmetic  39.5 us (8%)
  local copies, waits for them, and re-layouts  25.4 us (5%)
  between operations  13.3 us (3%)
    all_gather x1, waiting for transfers between devices, body(): lax.all_gather(w_key, 'ctx', axis=0, tiled=True)  127 us
    all_gather x1, waiting for transfers between devices, body(): lax.all_gather(w_value, 'ctx', axis=0, tiled=True)  116 us
    dot_general x4, matrix products, update(): jnp.einsum('tkgs,skd->tkgd', weights.astype(jnp.bfloat16), value_block, p...  52 us
    all_gather x1, waiting for transfers between devices, body(): value_piece = lax.all_gather(values, 'ctx', axis=0, tiled=True)  38.3 us
    reduce_sum x4, other arithmetic, update(): totals = totals * rescale + jnp.sum(weights, axis=-1)  31.9 us
    dot_general x4, matrix products, update(): jnp.einsum('tkgd,skd->tkgs', grouped_query, key_block, preferred_element_...  28.4 us
    all_gather x1, waiting for transfers between devices, body(): key_piece = lax.all_gather(keys, 'ctx', axis=0, tiled=True)  26 us
    dot_general x1, matrix products, body(): jnp.dot(normed, lax.all_gather(w_value, 'ctx', axis=0, tiled=True), prefe...  10.1 us
  transfers between devices with their start and end apart: 4, of which 4 were waited for; matrix products, arithmetic and copies ran while one was open for 7% of the time, Pallas kernels for 0%

commit v1 on v0

v1 whole, which is shorter than its diff:
```python
import functools
import math

import jax
import jax.numpy as jnp
from jax import lax
from jax.experimental import pallas as pl
from jax.experimental.pallas import tpu as pltpu
from jax.sharding import PartitionSpec as P

HD = 128
MESH = pl.DeviceIdType.MESH


def project_kernel(
    G, Q, Z, hidden_ref, gain_ref, wk_ref, wv_ref, cos_ref, sin_ref, kv_ref,
    send_x, xs, wbuf, acc, pair_buf, part_buf,
    xs_send, xs_recv, w_send, w_recv, pair_send, pair_recv, part_send, part_recv,
    kv_send, kv_recv,
):
    rows, width = hidden_ref.shape
    feats = wk_ref.shape[0]
    fg = feats // G
    kw = wk_ref.shape[1]
    S = G * Q
    g = lax.axis_index("groups")
    c = lax.axis_index("ctx")
    z = c // Q
    i = c % Q
    me = g * Q + i
    right = lax.rem(z + 1, Z) * Q + i
    left = lax.rem(z + Z - 1, Z) * Q + i

    def plane(s):
        return (s // Q, z * Q + s % Q)

    barrier = pltpu.get_barrier_semaphore()
    for r in range(1, S):
        pl.semaphore_signal(barrier, inc=1, device_id=plane(lax.rem(me + r, S)), device_id_type=MESH)
    pl.semaphore_signal(barrier, inc=1, device_id=(g, right), device_id_type=MESH)
    pl.semaphore_signal(barrier, inc=1, device_id=(g, left), device_id_type=MESH)
    pl.semaphore_wait(barrier, S + 1)

    def weight_copy(step, j):
        origin = lax.rem(z + Z - step, Z)
        if step == 0:
            src = (wk_ref, wv_ref)[j].at[pl.ds(pl.multiple_of(g * fg, fg), fg)]
        else:
            src = wbuf.at[origin, j]
        return pltpu.make_async_remote_copy(
            src_ref=src, dst_ref=wbuf.at[origin, j],
            send_sem=w_send.at[step, j], recv_sem=w_recv.at[step, j],
            device_id=(g, right), device_id_type=MESH,
        )

    w_copies = [[weight_copy(step, j) for j in range(2)] for step in range(Z - 1)]
    for j in range(2):
        w_copies[0][j].start()

    piece = 1024
    def square(t, total):
        part = hidden_ref[:, pl.ds(pl.multiple_of(t * piece, piece), piece)].astype(jnp.float32)
        part = part * part
        out = total
        for u in range(piece // 128):
            out = out + part[:, u * 128:(u + 1) * 128]
        return out
    total = lax.fori_loop(0, width // piece, square, jnp.zeros((rows, 128), jnp.float32))
    scale = lax.rsqrt(jnp.sum(total, axis=1, keepdims=True) / width + 1e-05)

    def normalise(s, dst, row0):
        sg = s // Q
        si = s % Q
        def one(zo, carry):
            col = pl.multiple_of((zo * Q + si) * feats + sg * fg, 128)
            h = hidden_ref[:, pl.ds(col, fg)].astype(jnp.float32)
            n = h * scale * gain_ref[:, pl.ds(col, fg)]
            dst[pl.ds(row0, rows), pl.ds(pl.multiple_of(zo * fg, 128), fg)] = n.astype(jnp.bfloat16)
            return carry
        lax.fori_loop(0, Z, one, 0)

    order = [S - 1] if S == 1 else list(range(S - 1, 0, -1))
    x_copies = []
    for r in order:
        s = lax.rem(me + r, S)
        normalise(s, send_x, (r - 1) * rows)
        copy = pltpu.make_async_remote_copy(
            src_ref=send_x.at[pl.ds((r - 1) * rows, rows)],
            dst_ref=xs.at[pl.ds(pl.multiple_of(me * rows, rows), rows)],
            send_sem=xs_send.at[r - 1], recv_sem=xs_recv.at[r - 1],
            device_id=plane(s), device_id_type=MESH,
        )
        copy.start()
        x_copies.append(copy)
    normalise(me, xs, pl.multiple_of(me * rows, rows))
    for r, copy in zip(order, x_copies):
        src = lax.rem(me + S - r, S)
        slot = xs.at[pl.ds(pl.multiple_of(src * rows, rows), rows)]
        pltpu.make_async_remote_copy(
            src_ref=slot, dst_ref=slot, send_sem=xs_send.at[r - 1], recv_sem=xs_recv.at[r - 1],
            device_id=plane(src), device_id_type=MESH,
        ).wait_recv()

    tile = 256
    for step in range(Z):
        origin = lax.rem(z + Z - step, Z)
        if step > 0:
            for j in range(2):
                slot = wbuf.at[origin, j]
                pltpu.make_async_remote_copy(
                    src_ref=slot, dst_ref=slot, send_sem=w_send.at[step - 1, j],
                    recv_sem=w_recv.at[step - 1, j], device_id=(g, right), device_id_type=MESH,
                ).wait_recv()
                if step < Z - 1:
                    w_copies[step][j].start()
        for j in range(2):
            def one(t, carry, step=step, j=j, origin=origin):
                at = pl.ds(pl.multiple_of(t * tile, tile), tile)
                if step == 0:
                    weight = (wk_ref, wv_ref)[j][pl.ds(pl.multiple_of(g * fg, fg), fg), :]
                else:
                    weight = wbuf[origin, j]
                product = jnp.dot(
                    xs[at, pl.ds(pl.multiple_of(origin * fg, 128), fg)], weight,
                    preferred_element_type=jnp.float32,
                )
                cols = pl.ds(j * kw, kw)
                if step == 0:
                    acc[at, cols] = product
                else:
                    acc[at, cols] = acc[at, cols] + product
                return carry
            lax.fori_loop(0, S * rows // tile, one, 0)

    half = S // 2
    core = me % 2
    other = me + 1 - 2 * core
    chip = me // 2
    pair_copies = []
    for r in range(half):
        t = lax.rem(chip + 1 + r, half)
        copy = pltpu.make_async_remote_copy(
            src_ref=acc.at[pl.ds(pl.multiple_of((2 * t + 1 - core) * rows, rows), rows)],
            dst_ref=pair_buf.at[t],
            send_sem=pair_send.at[r], recv_sem=pair_recv.at[r],
            device_id=plane(other), device_id_type=MESH,
        )
        copy.start()
        pair_copies.append(copy)
    part_copies = []
    for r in range(half):
        t = lax.rem(chip + 1 + r, half)
        slot = pair_buf.at[t]
        pltpu.make_async_remote_copy(
            src_ref=slot, dst_ref=slot, send_sem=pair_send.at[r], recv_sem=pair_recv.at[r],
            device_id=plane(other), device_id_type=MESH,
        ).wait_recv()
        mine = pl.ds(pl.multiple_of((2 * t + core) * rows, rows), rows)
        pair_buf[t] = pair_buf[t] + acc[mine, :]
        if r < half - 1:
            copy = pltpu.make_async_remote_copy(
                src_ref=pair_buf.at[t], dst_ref=part_buf.at[r],
                send_sem=part_send.at[r], recv_sem=part_recv.at[r],
                device_id=plane(2 * t + core), device_id_type=MESH,
            )
            copy.start()
            part_copies.append(copy)
    raw = pair_buf[chip]
    for r in range(half - 1):
        part_copies[r].wait_recv()
        raw = raw + part_buf[r]

    cosine = cos_ref[...]
    sine = sin_ref[...]
    for h in range(kw // HD):
        u = raw[:, h * HD:(h + 1) * HD]
        swapped = pltpu.roll(u, HD // 2, 1)
        kv_ref[c, :, h * HD:(h + 1) * HD] = (u * cosine + swapped * sine).astype(jnp.bfloat16)
    kv_ref[c, :, kw:] = raw[:, kw:].astype(jnp.bfloat16)

    def hop(origin, device, stage, k):
        return pltpu.make_async_remote_copy(
            src_ref=kv_ref.at[origin], dst_ref=kv_ref.at[origin],
            send_sem=kv_send.at[stage, k], recv_sem=kv_recv.at[stage, k],
            device_id=(g, device), device_id_type=MESH,
        )

    bits = []
    bit = Q // 2
    while bit >= 1:
        bits.append(bit)
        bit //= 2

    def peer(bit):
        return c + bit - 2 * bit * ((i // bit) % 2)

    sent = []
    counts = [0] * (len(bits) + 1)

    def fan(origin, stage):
        for b in range(stage, len(bits)):
            k = counts[b + 1]
            counts[b + 1] += 1
            copy = hop(origin, peer(bits[b]), b + 1, k)
            copy.start()
            sent.append(copy)

    arrivals = {b: [] for b in range(len(bits))}
    for step in range(Z):
        origin = lax.rem(z + Z - step, Z) * Q + i
        if step > 0:
            hop(origin, right, 0, step - 1).wait_recv()
        if step < Z - 1:
            copy = hop(origin, right, 0, step)
            copy.start()
            sent.append(copy)
        fan(origin, 0)
    held = [lax.rem(z + Z - step, Z) * Q + i for step in range(Z)]
    for b, bit in enumerate(bits):
        flip = bit - 2 * bit * ((i // bit) % 2)
        fresh = []
        for k, origin in enumerate(held):
            came = origin + flip
            hop(came, peer(bit), b + 1, k).wait_recv()
            fan(came, b + 1)
            fresh.append(came)
        held = held + fresh

    for step in range(Z - 1):
        for j in range(2):
            w_copies[step][j].wait_send()
    for copy in x_copies + pair_copies + part_copies + sent:
        copy.wait_send()


def project(G, Q, Z, hidden, gain, w_key, w_value, cosine, sine):
    rows, width = hidden.shape
    feats, kw = w_key.shape
    S = G * Q
    n = Z * Q
    fg = feats // G
    half = S // 2
    nbits = Q.bit_length() - 1
    dma = pltpu.SemaphoreType.DMA
    vm = pl.BlockSpec(memory_space=pltpu.VMEM)
    return pl.pallas_call(
        functools.partial(project_kernel, G, Q, Z),
        out_shape=jax.ShapeDtypeStruct((n, rows, 2 * kw), jnp.bfloat16),
        in_specs=[vm] * 6,
        out_specs=vm,
        scratch_shapes=[
            pltpu.VMEM(((S - 1) * rows, Z * fg), jnp.bfloat16),
            pltpu.VMEM((S * rows, Z * fg), jnp.bfloat16),
            pltpu.VMEM((Z, 2, fg, kw), jnp.bfloat16),
            pltpu.VMEM((S * rows, 2 * kw), jnp.float32),
            pltpu.VMEM((half, rows, 2 * kw), jnp.float32),
            pltpu.VMEM((half - 1, rows, 2 * kw), jnp.float32),
            dma((S - 1,)), dma((S - 1,)),
            dma((Z - 1, 2)), dma((Z - 1, 2)),
            dma((half,)), dma((half,)),
            dma((half - 1,)), dma((half - 1,)),
            dma((nbits + 1, n)), dma((nbits + 1, n)),
        ],
        compiler_params=pltpu.CompilerParams(
            collective_id=0, has_side_effects=True, vmem_limit_bytes=52 * 1024 * 1024
        ),
        name="project",
    )(hidden, gain, w_key, w_value, cosine, sine)


def attend_kernel(heads, coeff, q_ref, k_ref, v_ref, bias_ref, out_ref, kt, eye):
    rows = q_ref.shape[0]

    @pl.when(pl.program_id(0) == 0)
    def _():
        kt[HD:, :] = bias_ref[...]
        a = lax.broadcasted_iota(jnp.int32, (rows, rows), 0)
        b = lax.broadcasted_iota(jnp.int32, (rows, rows), 1)
        eye[...] = jnp.where(a == b, 1.0, 0.0).astype(jnp.bfloat16)

    kt[:HD, :] = k_ref[...].T
    ident = eye[...]

    def pair(p):
        col = p * 2 * HD
        top = jnp.concatenate([q_ref[:, col:col + HD], ident], axis=1)
        low = jnp.concatenate([q_ref[:, col + HD:col + 2 * HD], ident], axis=1)
        q = jnp.concatenate([top, low], axis=0)
        s = jnp.dot(q, kt[...], preferred_element_type=jnp.float32)
        m = jnp.max(s, axis=1, keepdims=True) * coeff
        w = jnp.exp2(s * coeff - m)
        total = jnp.sum(w, axis=1, keepdims=True)
        o = jnp.dot(w.astype(jnp.bfloat16), v_ref[...], preferred_element_type=jnp.float32)
        o = (o / total).astype(jnp.bfloat16)
        out_ref[:, col:col + HD] = o[:rows]
        out_ref[:, col + HD:col + 2 * HD] = o[rows:]

    for p in range(heads // 2):
        pair(p)


def attend(query, kv, bias, kv_heads):
    rows, qw = query.shape
    keys = kv.shape[0]
    heads = qw // HD // kv_heads
    coeff = math.log2(math.e) / math.sqrt(HD)
    return pl.pallas_call(
        functools.partial(attend_kernel, heads, coeff),
        grid=(kv_heads,),
        out_shape=jax.ShapeDtypeStruct((rows, qw), jnp.bfloat16),
        in_specs=[
            pl.BlockSpec((rows, heads * HD), lambda h: (0, h)),
            pl.BlockSpec((keys, HD), lambda h: (0, h)),
            pl.BlockSpec((keys, HD), lambda h: (0, kv_heads + h)),
            pl.BlockSpec((rows, keys), lambda h: (0, 0)),
        ],
        out_specs=pl.BlockSpec((rows, heads * HD), lambda h: (0, h)),
        scratch_shapes=[
            pltpu.VMEM((HD + rows, keys), jnp.bfloat16),
            pltpu.VMEM((rows, rows), jnp.bfloat16),
        ],
        compiler_params=pltpu.CompilerParams(vmem_limit_bytes=52 * 1024 * 1024),
        name="attend",
    )(query, kv, kv, bias)


def body(G, Q, Z, hidden, norm_gain, w_key, w_value, query, block_order):
    rows = hidden.shape[0]
    half_rows = rows // 2
    kv_heads = w_key.shape[1] // HD
    device = lax.axis_index("ctx")
    local = jnp.arange(half_rows, dtype=jnp.int32)
    key_positions = (block_order[:, None] * half_rows + local[None, :]).reshape(-1)
    own = lax.dynamic_slice_in_dim(block_order, 2 * device, 2)
    positions = (own[:, None] * half_rows + local[None, :]).reshape(-1)
    freqs = jnp.exp(
        jnp.arange(HD // 2, dtype=jnp.float32) * (-2.0 * math.log(500000.0) / HD)
    )
    angles = positions.astype(jnp.float32)[:, None] * freqs[None, :]
    cosine = jnp.cos(angles)
    sine = jnp.sin(angles)
    kv = project(
        G, Q, Z, hidden, norm_gain[None, :], w_key, w_value,
        jnp.concatenate([cosine, cosine], axis=1), jnp.concatenate([-sine, sine], axis=1),
    )
    bias = jnp.where(key_positions[None, :] <= positions[:, None], 0.0, -1e30).astype(jnp.bfloat16)
    return attend(query, kv.reshape(-1, kv.shape[2]), bias, kv_heads)


def solution(mesh):
    G = mesh.shape["groups"]
    n = mesh.shape["ctx"]
    Q = 8 // G
    return jax.shard_map(
        functools.partial(body, G, Q, n // Q),
        mesh=mesh,
        in_specs=(
            P(("groups", "ctx"), None),
            P(),
            P("ctx", None),
            P("ctx", None),
            P(("groups", "ctx"), None),
            P("groups"),
        ),
        out_specs=P(("groups", "ctx"), None),
        check_vma=False,
    )
```

time: 488 us -> 191 us (0.39)
  waiting for transfers between devices: 309 us -> 0 us
  Pallas kernels: 0 us -> 187 us
  matrix products: 99.9 us -> 0 us
  other arithmetic: 39.5 us -> 2.11 us
  local copies, waits for them, and re-layouts: 25.4 us -> 2.22 us
  between operations: 13.3 us -> 0.05 us
    all_gather x4 -> x0, waiting for transfers between devices: 307 us -> none  [the longest x1 127 us: body(): lax.all_gather(w_key, 'ctx', axis=0, tiled=True)]
    pallas_call x0 -> x2, Pallas kernels: none -> 187 us  [the longest x1 157 us: project(): pl.pallas_call(functools.partial(project_kernel, G, Q, Z), out_shape=jax....]
    dot_general x10 -> x0, matrix products: 99.9 us -> none  [the longest x4 52 us: update(): jnp.einsum('tkgs,skd->tkgd', weights.astype(jnp.bfloat16), value_block, p...]
    reduce_sum x7 -> x0, other arithmetic: 35.2 us -> none  [the longest x4 31.9 us: update(): totals = totals * rescale + jnp.sum(weights, axis=-1)]
    reshape x4 -> x0, local copies, waits for them, and re-layouts: 10.9 us -> none  [the longest x1 3.96 us: body(): value_blocks = value_piece.reshape(blocks, block_width, kv_heads, HD)]
    dynamic_slice x13 -> x0, local copies, waits for them, and re-layouts: 8.31 us -> none  [the longest x12 7.57 us: body(): lax.scan(advance, state_now, (key_blocks, value_blocks, position_blocks))]
  transfers between devices with their start and end apart: 4 -> 0, of which waited for: 4 -> 0; matrix products, arithmetic and copies ran while one was open for 7% -> 0% of each run, Pallas kernels for 0% -> 0%
where the time goes in v1:
time: 191 us
  Pallas kernels  187 us (98%)
  local copies, waits for them, and re-layouts  2.22 us (1%)
  other arithmetic  2.11 us (1%)
    pallas_call x1, Pallas kernels, project(): pl.pallas_call(functools.partial(project_kernel, G, Q, Z), out_shape=jax....  157 us
    pallas_call x1, Pallas kernels, attend(): pl.pallas_call(functools.partial(attend_kernel, heads, coeff), grid=(kv_h...  29.7 us

profile of v1, /device:TPU:0, one launch (start us, length us, event | category | flops | bytes accessed | tf_op | source)
XLA Modules:
  0.0 190.9 jit_solution(4814382869849576074)
XLA Ops:
  0.0 0.7 dynamic-slice_multiply_fusion
  0.7 0.1 iota_add_fusion.1
  0.8 0.1 add.51
  0.9 0.7 broadcast_multiply_fusion
  1.6 0.1 iota_add_fusion
  1.6 0.1 add.55
  1.7 0.3 fusion
  2.0 0.1 pad_maximum_fusion
  2.1 0.2 select_convert_fusion.bias_ref
  2.3 0.0 copy-start
  2.3 1.2 copy-done
  3.5 0.0 copy-start.1
  3.5 0.8 copy-done.1
  4.4 156.9 %project.1 = bf16[16,128,1024]{2,1,0:T(8,128)(2,1)} custom-call(bf16[128,16384]{1,0:T(8,128)(2,1)} %hidden_ref.1, f32[1,16384]{1,0:T(1,128)S(1)} %bitcast.2, bf16[1024,512]{1,0:T(8,128)(2,1)S(1)} %copy-done, bf16[1024,512]{1,0:T(8,128)(2,1)} %wv_ref.1, f32[128,128]{1,0:T(8,128)S(1)} %get-tuple-element.8.cos_ref, f32[128,128]{1,0:T(8,128)S(1)} %get-tuple-element.9.sin_ref), custom_call_target="tpu_custom_call" | custom-call | tf_op jit(solution)/shard_map/project/pallas_call | solution.py:246
  161.2 29.7 %attend.1 = bf16[128,8192]{1,0:T(8,128)(2,1)} custom-call(bf16[128,8192]{1,0:T(8,128)(2,1)} %q_ref.1, bf16[2048,1024]{1,0:T(8,128)(2,1)} %bitcast.3, bf16[2048,1024]{1,0:T(8,128)(2,1)} %bitcast.4, bf16[128,2048]{1,0:T(8,128)(2,1)S(1)} %select_convert_fusion.bias_ref), custom_call_target="tpu_custom_call" | custom-call | tf_op jit(solution)/shard_map/attend/pallas_call | solution.py:307
  (2 shorter events, 0.0 us)
Async XLA Ops:
  2.3 1.2 copy-start
  3.5 0.8 copy-start.1

commit v2 on v1

--- a/solution.py
+++ b/solution.py
@@ -93,6 +93,20 @@
         copy.start()
         x_copies.append(copy)
     normalise(me, xs, pl.multiple_of(me * rows, rows))
+
+    def weight_arrives(step):
+        origin = lax.rem(z + Z - step, Z)
+        for j in range(2):
+            slot = wbuf.at[origin, j]
+            pltpu.make_async_remote_copy(
+                src_ref=slot, dst_ref=slot, send_sem=w_send.at[step - 1, j],
+                recv_sem=w_recv.at[step - 1, j], device_id=(g, right), device_id_type=MESH,
+            ).wait_recv()
+            if step < Z - 1:
+                w_copies[step][j].start()
+
+    for step in range(1, Z - 1):
+        weight_arrives(step)
     for r, copy in zip(order, x_copies):
         src = lax.rem(me + S - r, S)
         slot = xs.at[pl.ds(pl.multiple_of(src * rows, rows), rows)]
@@ -104,15 +118,8 @@
     tile = 256
     for step in range(Z):
         origin = lax.rem(z + Z - step, Z)
-        if step > 0:
-            for j in range(2):
-                slot = wbuf.at[origin, j]
-                pltpu.make_async_remote_copy(
-                    src_ref=slot, dst_ref=slot, send_sem=w_send.at[step - 1, j],
-                    recv_sem=w_recv.at[step - 1, j], device_id=(g, right), device_id_type=MESH,
-                ).wait_recv()
-                if step < Z - 1:
-                    w_copies[step][j].start()
+        if step == Z - 1:
+            weight_arrives(step)
         for j in range(2):
             def one(t, carry, step=step, j=j, origin=origin):
                 at = pl.ds(pl.multiple_of(t * tile, tile), tile)

time: 191 us -> 174 us (0.911)
  Pallas kernels: 187 us -> 169 us
    pallas_call x1, Pallas kernels: 157 us -> 140 us  [project(): pl.pallas_call(functools.partial(project_kernel, G, Q, Z), out_shape=jax....]
where the time goes in v2:
time: 174 us
  Pallas kernels  169 us (97%)
  local copies, waits for them, and re-layouts  2.22 us (1%)
  other arithmetic  2.11 us (1%)
    pallas_call x1, Pallas kernels, project(): pl.pallas_call(functools.partial(project_kernel, G, Q, Z), out_shape=jax....  140 us
    pallas_call x1, Pallas kernels, attend(): pl.pallas_call(functools.partial(attend_kernel, heads, coeff), grid=(kv_h...  29.7 us

profile of v2, /device:TPU:0, one launch (start us, length us, event | category | flops | bytes accessed | tf_op | source)
XLA Modules:
  0.0 173.7 jit_solution(8968037841606940684)
XLA Ops:
  0.0 0.7 dynamic-slice_multiply_fusion
  0.7 0.1 iota_add_fusion.1
  0.8 0.1 add.51
  0.9 0.7 broadcast_multiply_fusion
  1.6 0.1 iota_add_fusion
  1.6 0.1 add.55
  1.7 0.3 fusion
  2.0 0.1 pad_maximum_fusion
  2.1 0.2 select_convert_fusion.bias_ref
  2.3 0.0 copy-start
  2.3 1.2 copy-done
  3.5 0.0 copy-start.1
  3.5 0.8 copy-done.1
  4.4 139.6 %project.1 = bf16[16,128,1024]{2,1,0:T(8,128)(2,1)} custom-call(bf16[128,16384]{1,0:T(8,128)(2,1)} %hidden_ref.1, f32[1,16384]{1,0:T(1,128)S(1)} %bitcast.2, bf16[1024,512]{1,0:T(8,128)(2,1)S(1)} %copy-done, bf16[1024,512]{1,0:T(8,128)(2,1)} %wv_ref.1, f32[128,128]{1,0:T(8,128)S(1)} %get-tuple-element.8.cos_ref, f32[128,128]{1,0:T(8,128)S(1)} %get-tuple-element.9.sin_ref), custom_call_target="tpu_custom_call" | custom-call | tf_op jit(solution)/shard_map/project/pallas_call | solution.py:253
  144.0 29.7 %attend.1 = bf16[128,8192]{1,0:T(8,128)(2,1)} custom-call(bf16[128,8192]{1,0:T(8,128)(2,1)} %q_ref.1, bf16[2048,1024]{1,0:T(8,128)(2,1)} %bitcast.3, bf16[2048,1024]{1,0:T(8,128)(2,1)} %bitcast.4, bf16[128,2048]{1,0:T(8,128)(2,1)S(1)} %select_convert_fusion.bias_ref), custom_call_target="tpu_custom_call" | custom-call | tf_op jit(solution)/shard_map/attend/pallas_call | solution.py:314
  (2 shorter events, 0.0 us)
Async XLA Ops:
  2.3 1.2 copy-start
  3.5 0.8 copy-start.1
